TPU v7x, 256 devices: a whole 4x4x8 slice. The times are simulated.
256 devices in a mesh: section: 2 (over z_hi), dp: 4 (over x), expert: 32 (over y, z_lo, core).
Axes of the slice: x: 4, y: 4, z: 8 (z_hi: 2, z_lo: 4; z = z_hi * 4 + z_lo), core: 2. Of those that a mesh axis runs over, the one named last changes fastest.
Arguments:
- activations: bfloat16 [2, 16384, 4096], P('section', ('dp', 'expert')), may hold values from -6 to 6
- norm_gain: float32 [2, 4096], P('section'), may hold values from 0.25 to 1.75
- route_ids: int32 [2, 16384, 2], P('section', ('dp', 'expert')), may hold values from 0 to 15, all different within a row; in each aligned block of 128 rows (0 to 127, 128 to 255, ..., all dimensions but the last counted through in order) at most 18 rows name the same one
- route_gates: float32 [2, 16384, 2], P('section', ('dp', 'expert')), may hold values from 0.2 to 1
- gate_weight: bfloat16 [2, 4096, 12288], P('section', None, 'expert'), may hold values from -0.09375 to 0.09375
- up_weight: bfloat16 [2, 4096, 12288], P('section', None, 'expert'), may hold values from -0.09375 to 0.09375
- leak_rates: float32 [2, 12288], P('section', 'expert'), may hold values from 0.2 to 0.9
- down_weight: bfloat16 [2, 12288, 4096], P('section', 'expert', 'dp'), may hold values from -0.21875 to 0.21875
- cotangent: bfloat16 [2, 16384, 4096], P('section', ('dp', 'expert')), may hold values from -6 to 6
Outputs:
- passed_on: bfloat16 [2, 16384, 4096], P('section', ('dp', 'expert'))
- passed_back: bfloat16 [2, 16384, 4096], P('section', ('dp', 'expert'))
- up_grad: bfloat16 [2, 4096, 12288], P('section', 'dp', 'expert')
Inputs may be any that keep to these rules, and one draw needn't show every extreme that they name: `route_ids`: within one section, the 128 tokens of one device name each expert at most 18 times, and some device reaches 18 for some expert; the two experts of a token differ.
All inputs are finite; a program needn't handle non-finite values.
Results may differ from a plain program's by a relative error of at most 0.015.
Values may be sent and summed in bfloat16 or wider, within the bound.
A program may use at most 192 MiB of HBM per device.

v0:
```python
import jax
import jax.numpy as jnp
from jax import lax
from jax.sharding import PartitionSpec as P

TSTEPS = 4
EPS = 1e-06
THETA = 0.5
SHARP = 4.0


def passed_along(value, axis, steps):
    count = lax.axis_size(axis)
    leading, last = (max(0, -steps), min(count, count - steps))
    return lax.ppermute(value, axis, [(source, source + steps) for source in range(leading, last)])


def lif_rate(gate_act, up_act, leak_rate):
    drive = jax.nn.silu(gate_act) * up_act
    volts = jnp.zeros_like(drive)
    spike_sum = jnp.zeros_like(drive)
    for timestep in range(TSTEPS):
        volts = leak_rate * volts + drive
        spikes = jax.nn.sigmoid(SHARP * (volts - THETA)) - jax.nn.sigmoid(SHARP * (-volts - THETA))
        volts = volts - THETA * spikes
        spike_sum = spike_sum + spikes
    return spike_sum / TSTEPS


def to_experts(slot_rows):
    model_width = slot_rows.shape[2]
    doubled = jnp.repeat(slot_rows, 2, axis=0)
    gathered = lax.all_to_all(doubled, "expert", split_axis=0, concat_axis=0, tiled=True)
    return gathered.reshape(-1, model_width)


def from_experts(partials, experts, capacity):
    model_width = partials.shape[2]
    returned = lax.all_to_all(
        partials.astype(jnp.bfloat16), "expert", split_axis=0, concat_axis=0, tiled=True
    ).astype(partials.dtype)
    paired = returned.reshape(experts, 2, capacity, model_width)
    summed = jnp.sum(paired, axis=1).astype(jnp.bfloat16)
    return summed.reshape(experts * capacity, model_width).astype(jnp.float32)


def per_device(
    activations,
    norm_gain,
    route_ids,
    route_gates,
    gate_weight,
    up_weight,
    leak_rates,
    down_weight,
    cotangent,
):
    tok_count = activations.shape[1]
    model_width = activations.shape[2]
    experts = lax.axis_size("expert") // 2
    capacity = min(tok_count, 2 * (9 * tok_count // (8 * experts)))
    tokens = activations[0].astype(jnp.float32)
    gain_row = norm_gain[0]
    inv_rms = lax.rsqrt(jnp.mean(tokens * tokens, axis=-1, keepdims=True) + EPS)
    normed = (tokens * inv_rms * gain_row).astype(jnp.bfloat16)
    flat_ids = route_ids[0].reshape(-1)
    onehot = (flat_ids[:, None] == jnp.arange(experts, dtype=jnp.int32)[None, :]).astype(jnp.int32)
    slot_index = jnp.sum(onehot * (jnp.cumsum(onehot, axis=0) - 1), axis=1)
    places = (flat_ids * capacity + slot_index).reshape(tok_count, 2)
    positions = jnp.arange(experts * capacity, dtype=jnp.int32)[:, None]
    pick_first = positions == places[None, :, 0]
    pick_second = positions == places[None, :, 1]
    pick_both = jnp.logical_or(pick_first, pick_second)
    slot_rows = jnp.dot(
        pick_both.astype(jnp.bfloat16), normed, preferred_element_type=jnp.float32
    ).astype(jnp.bfloat16)
    arrived = to_experts(slot_rows.reshape(experts, capacity, model_width))
    gate_local = gate_weight[0]
    up_local = up_weight[0]
    leak_local = leak_rates[0]
    down_full = lax.all_gather(down_weight[0], "dp", axis=1, tiled=True)
    gate_act = jnp.dot(arrived, gate_local, preferred_element_type=jnp.float32)
    up_act = jnp.dot(arrived, up_local, preferred_element_type=jnp.float32)
    spike_rate = lif_rate(gate_act, up_act, leak_local).astype(jnp.bfloat16)
    out_part = jnp.dot(spike_rate, down_full, preferred_element_type=jnp.float32)
    expert_out = from_experts(out_part.reshape(-1, capacity, model_width), experts, capacity)
    weights = route_gates[0]
    mixing = jnp.where(pick_first.T, weights[:, 0:1], 0.0) + jnp.where(
        pick_second.T, weights[:, 1:2], 0.0
    )
    moe_sum = jnp.dot(
        mixing, expert_out, precision=lax.Precision.HIGHEST, preferred_element_type=jnp.float32
    )
    section_out = (tokens + moe_sum).astype(jnp.bfloat16)
    passed_on = passed_along(section_out[None], "section", 1)
    upstream = cotangent[0].astype(jnp.float32)
    grad_first = (weights[:, 0:1] * upstream).astype(jnp.bfloat16)
    grad_second = (weights[:, 1:2] * upstream).astype(jnp.bfloat16)
    grad_slots = jnp.dot(
        pick_first.astype(jnp.bfloat16), grad_first, preferred_element_type=jnp.float32
    )
    grad_slots = grad_slots + jnp.dot(
        pick_second.astype(jnp.bfloat16), grad_second, preferred_element_type=jnp.float32
    )
    grad_rows = to_experts(grad_slots.astype(jnp.bfloat16).reshape(experts, capacity, model_width))
    rate_grad = lax.dot_general(
        grad_rows, down_full, (((1,), (1,)), ((), ())), preferred_element_type=jnp.float32
    )
    unused_rate, pullback = jax.vjp(
        lambda gate_in, up_in: lif_rate(gate_in, up_in, leak_local), gate_act, up_act
    )
    gate_grad, up_act_grad = pullback(rate_grad)
    gate_grad = gate_grad.astype(jnp.bfloat16)
    up_act_grad = up_act_grad.astype(jnp.bfloat16)
    back_part = lax.dot_general(
        gate_grad, gate_local, (((1,), (1,)), ((), ())), preferred_element_type=jnp.float32
    )
    back_part = back_part + lax.dot_general(
        up_act_grad, up_local, (((1,), (1,)), ((), ())), preferred_element_type=jnp.float32
    )
    route_back = from_experts(back_part.reshape(-1, capacity, model_width), experts, capacity)
    norm_grad = (
        jnp.dot(
            pick_both.T.astype(jnp.float32),
            route_back,
            precision=lax.Precision.HIGHEST,
            preferred_element_type=jnp.float32,
        )
        * gain_row
    )
    section_back = (
        upstream
        + inv_rms * norm_grad
        - tokens
        * (inv_rms * inv_rms * inv_rms)
        * jnp.mean(tokens * norm_grad, axis=-1, keepdims=True)
    )
    passed_back = passed_along(section_back.astype(jnp.bfloat16)[None], "section", -1)
    up_term = lax.dot_general(
        arrived, up_act_grad, (((0,), (0,)), ((), ())), preferred_element_type=jnp.float32
    )
    up_term = up_term.astype(jnp.bfloat16).astype(jnp.float32)
    up_grad = lax.psum_scatter(up_term.astype(jnp.bfloat16), "dp", scatter_dimension=0, tiled=True)[
        None
    ]
    return (passed_on, passed_back, up_grad)


def solution(mesh):
    return jax.shard_map(
        per_device,
        mesh=mesh,
        in_specs=(
            P("section", ("dp", "expert"), None),
            P("section", None),
            P("section", ("dp", "expert"), None),
            P("section", ("dp", "expert"), None),
            P("section", None, "expert"),
            P("section", None, "expert"),
            P("section", "expert"),
            P("section", "expert", "dp"),
            P("section", ("dp", "expert"), None),
        ),
        out_specs=(
            P("section", ("dp", "expert"), None),
            P("section", ("dp", "expert"), None),
            P("section", "dp", "expert"),
        ),
        check_vma=False,
    )
```

profile of v0, /device:TPU:73, one launch (start us, length us, event | category | flops | bytes accessed | tf_op | source)
XLA Modules:
  0.0 713.4 jit_solution(17626897167263078738)
XLA Ops:
  11.2 3.5 convolution_convert_fusion.2
  14.7 4.3 reshape.95
  19.0 5.3 broadcast_in_dim.46
  24.4 8.7 %all-to-all-start = ((bf16[32,18,4096]{2,1,0:T(8,128)(2,1)}), bf16[32,18,4096]{2,1,0:T(8,128)(2,1)}, u32[]{:S(2)}, u32[]{:S(2)}) async-start(bf16[32,18,4096]{2,1,0:T(8,128)(2,1)} %bitcast.85), calls=%async_computation | async-start | bytes 12582912 | tf_op jit(solution)/shard_map/all_to_all | solution.py:33
  37.6 4.3 reshape.100
  42.0 127.4 %all-to-all-done = bf16[32,18,4096]{2,1,0:T(8,128)(2,1)} async-done(((bf16[32,18,4096]{2,1,0:T(8,128)(2,1)}), bf16[32,18,4096]{2,1,0:T(8,128)(2,1)}, u32[]{:S(2)}, u32[]{:S(2)}) %all-to-all-start) | async-done | bytes 4718624 | tf_op jit(solution)/shard_map/all_to_all | solution.py:33
  169.4 5.3 broadcast_in_dim.48
  174.6 9.1 %all-to-all-start.2 = ((bf16[32,18,4096]{2,1,0:T(8,128)(2,1)}), bf16[32,18,4096]{2,1,0:T(8,128)(2,1)}, u32[]{:S(2)}, u32[]{:S(2)}) async-start(bf16[32,18,4096]{2,1,0:T(8,128)(2,1)} %bitcast.84), calls=%async_computation.2 | async-start | bytes 12582912 | tf_op jit(solution)/shard_map/all_to_all | solution.py:33
  184.5 7.7 %reshape.97 = bf16[576,4096]{1,0:T(8,128)(2,1)} reshape(bf16[32,18,4096]{2,1,0:T(8,128)(2,1)} %all-to-all-done) | data formatting | bytes 9437184 | tf_op jit(solution)/shard_map/reshape | solution.py:34
  192.2 7.0 fusion.7
  199.2 3.5 fusion.11
  202.7 25.7 %all-gather.3.cloned.1.call-done = bf16[1,384,4096]{2,1,0:T(8,128)(2,1)} async-done(((bf16[1,384,1024]{2,1,0:T(8,128)(2,1)}), bf16[1,384,4096]{2,1,0:T(8,128)(2,1)}) %all-gather.3.cloned.1.call-update) | async-done | bytes 3145744 | tf_op jit(solution)/shard_map/all_gather | solution.py:81
  228.5 9.4 %convolution_convert_fusion = bf16[576,4096]{1,0:T(8,128)(2,1)} fusion(bf16[1,384,4096]{2,1,0:T(8,128)(2,1)} %all-gather.3.cloned.1.call-done, f32[384]{0:T(512)S(1)} %reduce.5, f32[384]{0:T(512)S(1)} %broadcast_multiply_fusion, f32[576,384]{1,0:T(8,128)} %fusion.7, f32[576,384]{1,0:T(8,128)} %fusion.11), kind=kOutput, calls=%fused_computation.3 | convolution fusion | flops 1830002688 | bytes 9636864 | tf_op jit(solution)/shard_map/dot_general | solution.py:85
  237.9 7.6 %convert_element_type.93 = bf16[32,18,4096]{2,1,0:T(8,128)(2,1)} reshape(bf16[576,4096]{1,0:T(8,128)(2,1)} %convolution_convert_fusion) | data formatting | bytes 9437184 | tf_op jit(solution)/shard_map/convert_element_type | solution.py:40
  245.5 74.4 %all-to-all-done.2 = bf16[32,18,4096]{2,1,0:T(8,128)(2,1)} async-done(((bf16[32,18,4096]{2,1,0:T(8,128)(2,1)}), bf16[32,18,4096]{2,1,0:T(8,128)(2,1)}, u32[]{:S(2)}, u32[]{:S(2)}) %all-to-all-start.2) | async-done | bytes 4718624 | tf_op jit(solution)/shard_map/all_to_all | solution.py:33
  320.0 9.7 %all-to-all-start.1 = ((bf16[32,18,4096]{2,1,0:T(8,128)(2,1)}), bf16[32,18,4096]{2,1,0:T(8,128)(2,1)}, u32[]{:S(2)}, u32[]{:S(2)}) async-start(bf16[32,18,4096]{2,1,0:T(8,128)(2,1)} %convert_element_type.93), calls=%async_computation.1 | async-start | bytes 12582912 | tf_op jit(solution)/shard_map/all_to_all | solution.py:39
  329.7 7.7 %reshape.102 = bf16[576,4096]{1,0:T(8,128)(2,1)} reshape(bf16[32,18,4096]{2,1,0:T(8,128)(2,1)} %all-to-all-done.2) | data formatting | bytes 9437184 | tf_op jit(solution)/shard_map/reshape | solution.py:34
  337.4 10.1 %multiply_convert_fusion = (bf16[576,384]{1,0:T(8,128)(2,1)S(1)}, f32[576,384]{1,0:T(8,128)S(1)}) fusion(f32[576,384]{1,0:T(8,128)} %fusion.11, f32[576,384]{1,0:T(8,128)} %fusion.7, f32[384]{0:T(512)S(1)} %broadcast_multiply_fusion, f32[384]{0:T(512)S(1)} %reduce.5, bf16[576,4096]{1,0:T(8,128)(2,1)} %reshape.102, ...), kind=kOutput, calls=%fused_computation.87 | convolution fusion | flops 1840693248 | bytes 10963968 | tf_op jit(solution)/shard_map/dot_general | solution.py:106
  350.3 4.3 add_convert_fusion
  354.6 7.6 %convert_element_type.105 = bf16[32,18,4096]{2,1,0:T(8,128)(2,1)} reshape(bf16[576,4096]{1,0:T(8,128)(2,1)} %add_convert_fusion) | data formatting | bytes 9437184 | tf_op jit(solution)/shard_map/convert_element_type | solution.py:40
  362.3 103.5 %all-to-all-done.1 = bf16[32,18,4096]{2,1,0:T(8,128)(2,1)} async-done(((bf16[32,18,4096]{2,1,0:T(8,128)(2,1)}), bf16[32,18,4096]{2,1,0:T(8,128)(2,1)}, u32[]{:S(2)}, u32[]{:S(2)}) %all-to-all-start.1) | async-done | bytes 4718624 | tf_op jit(solution)/shard_map/all_to_all | solution.py:39
  465.7 9.0 %all-to-all-start.3 = ((bf16[32,18,4096]{2,1,0:T(8,128)(2,1)}), bf16[32,18,4096]{2,1,0:T(8,128)(2,1)}, u32[]{:S(2)}, u32[]{:S(2)}) async-start(bf16[32,18,4096]{2,1,0:T(8,128)(2,1)} %convert_element_type.105), calls=%async_computation.3 | async-start | bytes 12582912 | tf_op jit(solution)/shard_map/all_to_all | solution.py:39
  475.0 7.3 %convolution_convert_fusion.1 = bf16[4096,384]{1,0:T(8,128)(2,1)} fusion(bf16[576,4096]{1,0:T(8,128)(2,1)} %reshape.97, bf16[576,384]{1,0:T(8,128)(2,1)} %copy-done.8), kind=kOutput, calls=%fused_computation.4 | convolution fusion | flops 1813512192 | bytes 8306688 | tf_op jit(solution)/shard_map/dot_general | solution.py:139
  482.4 6.8 bitcast_reduce_fusion.1
  489.2 4.3 convert_element_type.95
  493.5 5.3 fusion.2
  498.8 7.0 collective-permute-start
  505.8 127.6 %all-to-all-done.3 = bf16[32,18,4096]{2,1,0:T(8,128)(2,1)} async-done(((bf16[32,18,4096]{2,1,0:T(8,128)(2,1)}), bf16[32,18,4096]{2,1,0:T(8,128)(2,1)}, u32[]{:S(2)}, u32[]{:S(2)}) %all-to-all-start.3) | async-done | bytes 4718624 | tf_op jit(solution)/shard_map/all_to_all | solution.py:39
  633.5 6.9 bitcast_reduce_fusion
  640.3 4.3 convert_element_type.107
  644.7 2.9 fusion.21
  649.8 52.0 %collective-permute-done.1 = bf16[1,128,4096]{2,1,0:T(8,128)(2,1)} collective-permute-done((bf16[1,128,4096]{2,1,0:T(8,128)(2,1)S(1)}, bf16[1,128,4096]{2,1,0:T(8,128)(2,1)}, u32[]{:S(2)}, u32[]{:S(2)}) %collective-permute-start.1) | collective-permute-done | bytes 1048608 | tf_op jit(solution)/shard_map/ppermute | solution.py:15
  (55 shorter events, 18.9 us)
Async XLA Ops:
  7.2 192.0 %copy-start = (bf16[1,4096,384]{2,1,0:T(8,128)(2,1)S(1)}, bf16[1,4096,384]{2,1,0:T(8,128)(2,1)}, u32[]{:S(2)}) copy-start(bf16[1,4096,384]{2,1,0:T(8,128)(2,1)} %param.13) | copy-start | bytes 9437188
  24.4 8.7 %copy-start.11 = (f32[1,128,2]{1,2,0:T(2,128)S(1)}, f32[1,128,2]{1,2,0:T(2,128)}, u32[]{:S(2)}) copy-start(f32[1,128,2]{1,2,0:T(2,128)} %param.12) | copy-start | bytes 3076
  24.4 145.0 %all-to-all-start = ((bf16[32,18,4096]{2,1,0:T(8,128)(2,1)}), bf16[32,18,4096]{2,1,0:T(8,128)(2,1)}, u32[]{:S(2)}, u32[]{:S(2)}) async-start(bf16[32,18,4096]{2,1,0:T(8,128)(2,1)} %bitcast.85), calls=%async_computation | async-start | bytes 12582912 | tf_op jit(solution)/shard_map/all_to_all | solution.py:33
  33.1 2.2 copy-start.2
  174.6 9.8 %copy-start.10 = (f32[1,384]{1,0:T(1,128)S(1)}, f32[1,384]{1,0:T(1,128)}, u32[]{:S(2)}) copy-start(f32[1,384]{1,0:T(1,128)} %param.15) | copy-start | bytes 4612
  174.6 145.3 %all-to-all-start.2 = ((bf16[32,18,4096]{2,1,0:T(8,128)(2,1)}), bf16[32,18,4096]{2,1,0:T(8,128)(2,1)}, u32[]{:S(2)}, u32[]{:S(2)}) async-start(bf16[32,18,4096]{2,1,0:T(8,128)(2,1)} %bitcast.84), calls=%async_computation.2 | async-start | bytes 12582912 | tf_op jit(solution)/shard_map/all_to_all | solution.py:33
  183.7 44.7 %all-gather.3.cloned.1.call-start = ((), (), s32[]{:S(2)}) async-start(), calls=%async_computation.6 | async-start | bytes 3932160 | tf_op jit(solution)/shard_map/all_gather | solution.py:81
  192.2 7.0 copy-start.4
  320.0 145.8 %all-to-all-start.1 = ((bf16[32,18,4096]{2,1,0:T(8,128)(2,1)}), bf16[32,18,4096]{2,1,0:T(8,128)(2,1)}, u32[]{:S(2)}, u32[]{:S(2)}) async-start(bf16[32,18,4096]{2,1,0:T(8,128)(2,1)} %convert_element_type.93), calls=%async_computation.1 | async-start | bytes 12582912 | tf_op jit(solution)/shard_map/all_to_all | solution.py:39
  337.4 10.1 %copy-start.6 = (f32[576,384]{1,0:T(8,128)S(1)}, f32[576,384]{1,0:T(8,128)}, u32[]{:S(2)}) copy-start(f32[576,384]{1,0:T(8,128)} %fusion.7) | copy-start | bytes 2654212
  337.4 10.2 %copy-start.7 = (f32[576,384]{1,0:T(8,128)S(1)}, f32[576,384]{1,0:T(8,128)}, u32[]{:S(2)}) copy-start(f32[576,384]{1,0:T(8,128)} %fusion.11) | copy-start | bytes 2654212
  347.6 2.8 copy-start.8
  347.6 2.7 copy-start.5
  465.7 167.7 %all-to-all-start.3 = ((bf16[32,18,4096]{2,1,0:T(8,128)(2,1)}), bf16[32,18,4096]{2,1,0:T(8,128)(2,1)}, u32[]{:S(2)}, u32[]{:S(2)}) async-start(bf16[32,18,4096]{2,1,0:T(8,128)(2,1)} %convert_element_type.105), calls=%async_computation.3 | async-start | bytes 12582912 | tf_op jit(solution)/shard_map/all_to_all | solution.py:39
  474.8 227.0 %reduce-scatter.2.cloned.1.call-start = ((), (), s32[]{:S(2)}) async-start(), calls=%async_computation.5 | async-start | bytes 3932160 | tf_op jit(solution)/shard_map/reduce_scatter | solution.py:143
  498.8 151.0 %collective-permute-start = (bf16[1,128,4096]{2,1,0:T(8,128)(2,1)}, bf16[1,128,4096]{2,1,0:T(8,128)(2,1)}, u32[]{:S(2)}, u32[]{:S(2)}) collective-permute-start(bf16[1,128,4096]{2,1,0:T(8,128)(2,1)} %fusion.2), channel_id=1, source_target_pairs={{0,128},{1,129},{2,130},{3,131},{4,132},{5,133},{6,134},{7,135},{8... | collective-permute-start | bytes 3145736 | tf_op jit(solution)/shard_map/ppermute | solution.py:15
  640.3 4.3 copy-start.9
  644.7 3.0 copy-start.1
  644.7 3.0 copy-start.3
  648.5 53.3 %collective-permute-start.1 = (bf16[1,128,4096]{2,1,0:T(8,128)(2,1)S(1)}, bf16[1,128,4096]{2,1,0:T(8,128)(2,1)}, u32[]{:S(2)}, u32[]{:S(2)}) collective-permute-start(bf16[1,128,4096]{2,1,0:T(8,128)(2,1)S(1)} %fusion.26), channel_id=1, source_target_pairs={{128,0},{129,1},{130,2},{131,3},{132,4},{133,5},{134,6},{135,7},{1... | collective-permute-start | bytes 3145736 | tf_op jit(solution)/shard_map/ppermute | solution.py:15
Sparse Core Ops, SparseCore 0:
  186.4 42.0 all-gather.2
  482.5 40.8 reduce-scatter.1
where the time goes:
time: 720 us; the launch traced here: 713 us
  waiting for transfers between devices  511 us (71%)
  local copies, waits for them, and re-layouts  65 us (9%)
  matrix products  60.6 us (8%)
  starting transfers between devices  45.4 us (6%)
  other arithmetic  16.8 us (2%)
  between operations  14.5 us (2%)
    all_to_all x2, waiting for transfers between devices, from_experts(): lax.all_to_all(partials.astype(jnp.bfloat16), 'expert', split_axis=0, con...  231 us
    all_to_all x2, waiting for transfers between devices, to_experts(): lax.all_to_all(doubled, 'expert', split_axis=0, concat_axis=0, tiled=True)  202 us
    ppermute x2, waiting for transfers between devices, passed_along(): lax.ppermute(value, axis, [(source, source + steps) for source in range(l...  52 us
    all_gather x1, waiting for transfers between devices, per_device(): down_full = lax.all_gather(down_weight[0], 'dp', axis=1, tiled=True)  25.7 us
    all_to_all x2, starting transfers between devices, from_experts(): lax.all_to_all(partials.astype(jnp.bfloat16), 'expert', split_axis=0, con...  18.7 us
    all_to_all x2, starting transfers between devices, to_experts(): lax.all_to_all(doubled, 'expert', split_axis=0, concat_axis=0, tiled=True)  17.8 us
    reshape x2, local copies, waits for them, and re-layouts, to_experts(): return gathered.reshape(-1, model_width)  15.5 us
    convert_element_type x2, local copies, waits for them, and re-layouts, from_experts(): partials.astype(jnp.bfloat16)  15.2 us
  transfers between devices with their start and end apart: 8, of which 6 were waited for; matrix products, arithmetic and copies ran while one was open for 16% of the time, Pallas kernels for 0%

commit v1 on v0

--- a/solution.py
+++ b/solution.py
@@ -1,3 +1,4 @@
+import functools
 import jax
 import jax.numpy as jnp
 from jax import lax
@@ -7,6 +8,16 @@
 EPS = 1e-06
 THETA = 0.5
 SHARP = 4.0
+
+
+def _set_ticks(tile_in, device_axis):
+    extra = jnp.concatenate(
+        lax.all_to_all(jnp.stack([tile_in] * lax.axis_size(device_axis)), device_axis, 0, 0), axis=1
+    )
+    return extra
+
+
+_match_roots = functools.partial(_set_ticks, device_axis="dp")
 
 
 def passed_along(value, axis, steps):
@@ -78,7 +89,7 @@
     gate_local = gate_weight[0]
     up_local = up_weight[0]
     leak_local = leak_rates[0]
-    down_full = lax.all_gather(down_weight[0], "dp", axis=1, tiled=True)
+    down_full = _match_roots(down_weight[0])
     gate_act = jnp.dot(arrived, gate_local, preferred_element_type=jnp.float32)
     up_act = jnp.dot(arrived, up_local, preferred_element_type=jnp.float32)
     spike_rate = lif_rate(gate_act, up_act, leak_local).astype(jnp.bfloat16)

time: 720 us -> 782 us (1.086)
  waiting for transfers between devices: 511 us -> 562 us
  local copies, waits for them, and re-layouts: 65 us -> 77 us
    all_to_all x2, waiting for transfers between devices: 202 us -> 241 us  [to_experts(): lax.all_to_all(doubled, 'expert', split_axis=0, concat_axis=0, tiled=True)]
    all_to_all x0 -> x1, waiting for transfers between devices: none -> 26 us  [_set_ticks(): lax.all_to_all(jnp.stack([tile_in] * lax.axis_size(device_axis)), device_...]
    all_gather x1 -> x0, waiting for transfers between devices: 25.7 us -> none  [per_device(): down_full = lax.all_gather(down_weight[0], 'dp', axis=1, tiled=True)]
    all_to_all x2, waiting for transfers between devices: 231 us -> 250 us  [from_experts(): lax.all_to_all(partials.astype(jnp.bfloat16), 'expert', split_axis=0, con...]
    reshape x0 -> x3, local copies, waits for them, and re-layouts: none -> 12.3 us  [_set_ticks(): jnp.concatenate(lax.all_to_all(jnp.stack([tile_in] * lax.axis_size(device...]
  transfers between devices with their start and end apart: 8 -> 8, of which waited for: 6 -> 6; matrix products, arithmetic and copies ran while one was open for 16% -> 12% of each run, Pallas kernels for 0% -> 0%
where the time goes in v1:
time: 782 us; the launch traced here: 774 us
  waiting for transfers between devices  562 us (72%)
  local copies, waits for them, and re-layouts  77 us (10%)
  matrix products  54.4 us (7%)
  starting transfers between devices  51.1 us (7%)
  other arithmetic  15.5 us (2%)
  between operations  14.5 us (2%)
    all_to_all x2, waiting for transfers between devices, from_experts(): lax.all_to_all(partials.astype(jnp.bfloat16), 'expert', split_axis=0, con...  250 us
    all_to_all x2, waiting for transfers between devices, to_experts(): lax.all_to_all(doubled, 'expert', split_axis=0, concat_axis=0, tiled=True)  241 us
    ppermute x2, waiting for transfers between devices, passed_along(): lax.ppermute(value, axis, [(source, source + steps) for source in range(l...  44.2 us
    all_to_all x1, waiting for transfers between devices, _set_ticks(): lax.all_to_all(jnp.stack([tile_in] * lax.axis_size(device_axis)), device_...  26 us
    all_to_all x2, starting transfers between devices, to_experts(): lax.all_to_all(doubled, 'expert', split_axis=0, concat_axis=0, tiled=True)  19.3 us
    all_to_all x2, starting transfers between devices, from_experts(): lax.all_to_all(partials.astype(jnp.bfloat16), 'expert', split_axis=0, con...  18.4 us
  transfers between devices with their start and end apart: 8, of which 6 were waited for; matrix products, arithmetic and copies ran while one was open for 12% of the time, Pallas kernels for 0%

profile of v1, /device:TPU:73, one launch (start us, length us, event | category | flops | bytes accessed | tf_op | source)
XLA Modules:
  0.0 774.2 jit_solution(9300133928581210448)
XLA Ops:
  10.5 4.8 all-to-all-start.1
  22.1 4.3 reshape.102
  26.4 26.0 %all-to-all-done.1 = bf16[4,384,1024]{2,1,0:T(8,128)(2,1)} async-done(((bf16[4,384,1024]{2,1,0:T(8,128)(2,1)}), bf16[4,384,1024]{2,1,0:T(8,128)(2,1)}, u32[]{:S(2)}, u32[]{:S(2)}) %all-to-all-start.1) | async-done | bytes 3145760 | tf_op jit(solution)/shard_map/all_to_all | solution.py:15
  52.4 5.3 broadcast_in_dim.46
  57.7 9.6 %all-to-all-start = ((bf16[32,18,4096]{2,1,0:T(8,128)(2,1)}), bf16[32,18,4096]{2,1,0:T(8,128)(2,1)}, u32[]{:S(2)}, u32[]{:S(2)}) async-start(bf16[32,18,4096]{2,1,0:T(8,128)(2,1)} %bitcast.79), calls=%async_computation | async-start | bytes 12582912 | tf_op jit(solution)/shard_map/all_to_all | solution.py:44
  71.9 4.3 reshape.109
  76.2 127.4 %all-to-all-done = bf16[32,18,4096]{2,1,0:T(8,128)(2,1)} async-done(((bf16[32,18,4096]{2,1,0:T(8,128)(2,1)}), bf16[32,18,4096]{2,1,0:T(8,128)(2,1)}, u32[]{:S(2)}, u32[]{:S(2)}) %all-to-all-start) | async-done | bytes 4718624 | tf_op jit(solution)/shard_map/all_to_all | solution.py:44
  203.6 5.3 broadcast_in_dim.48
  208.9 9.7 %all-to-all-start.3 = ((bf16[32,18,4096]{2,1,0:T(8,128)(2,1)}), bf16[32,18,4096]{2,1,0:T(8,128)(2,1)}, u32[]{:S(2)}, u32[]{:S(2)}) async-start(bf16[32,18,4096]{2,1,0:T(8,128)(2,1)} %bitcast.80), calls=%async_computation.3 | async-start | bytes 12582912 | tf_op jit(solution)/shard_map/all_to_all | solution.py:44
  218.6 4.0 copy.34
  222.6 7.7 reshape.104
  230.4 7.0 fusion.4
  240.9 113.8 %all-to-all-done.3 = bf16[32,18,4096]{2,1,0:T(8,128)(2,1)} async-done(((bf16[32,18,4096]{2,1,0:T(8,128)(2,1)}), bf16[32,18,4096]{2,1,0:T(8,128)(2,1)}, u32[]{:S(2)}, u32[]{:S(2)}) %all-to-all-start.3) | async-done | bytes 4718624 | tf_op jit(solution)/shard_map/all_to_all | solution.py:44
  354.6 7.7 reshape.111
  362.4 10.3 %multiply_convert_fusion = (bf16[576,384]{1,0:T(8,128)(2,1)S(1)}, bf16[576,384]{1,0:T(8,128)(2,1)}, f32[576,384]{1,0:T(8,128)S(1)}) fusion(f32[576,384]{1,0:T(8,128)} %fusion.8, f32[384]{0:T(512)S(1)} %reduce.5, f32[576,384]{1,0:T(8,128)} %fusion.4, f32[384]{0:T(512)S(1)} %broadcast_multiply_fusion, bf16[576,4096]{1,0:T(8,128)(2,1)} %reshape.111, ...), kind=kOutput, calls=%fused_computation.84 | convolution fusion | flops 1842020352 | bytes 11406336 | tf_op jit(solution)/shard_map/dot_general | solution.py:117
  375.5 4.3 add_convert_fusion
  379.8 7.6 convert_element_type.101
  387.4 9.4 %all-to-all-start.4 = ((bf16[32,18,4096]{2,1,0:T(8,128)(2,1)}), bf16[32,18,4096]{2,1,0:T(8,128)(2,1)}, u32[]{:S(2)}, u32[]{:S(2)}) async-start(bf16[32,18,4096]{2,1,0:T(8,128)(2,1)} %convert_element_type.101), calls=%async_computation.4 | async-start | bytes 12582912 | tf_op jit(solution)/shard_map/all_to_all | solution.py:50
  396.8 4.3 copy.27
  401.1 4.0 reshape.116
  406.3 4.7 convolution_convert_fusion
  411.0 5.4 copy.29
  416.4 116.5 %all-to-all-done.4 = bf16[32,18,4096]{2,1,0:T(8,128)(2,1)} async-done(((bf16[32,18,4096]{2,1,0:T(8,128)(2,1)}), bf16[32,18,4096]{2,1,0:T(8,128)(2,1)}, u32[]{:S(2)}, u32[]{:S(2)}) %all-to-all-start.4) | async-done | bytes 4718624 | tf_op jit(solution)/shard_map/all_to_all | solution.py:50
  532.8 9.0 %all-to-all-start.2 = ((bf16[32,18,4096]{2,1,0:T(8,128)(2,1)}), bf16[32,18,4096]{2,1,0:T(8,128)(2,1)}, u32[]{:S(2)}, u32[]{:S(2)}) async-start(bf16[32,18,4096]{2,1,0:T(8,128)(2,1)} %copy.29), calls=%async_computation.2 | async-start | bytes 12582912 | tf_op jit(solution)/shard_map/all_to_all | solution.py:50
  542.1 7.3 convolution_convert_fusion.1
  549.4 6.9 bitcast_reduce_fusion
  556.3 4.6 convert_element_type.103
  566.7 133.9 %all-to-all-done.2 = bf16[32,18,4096]{2,1,0:T(8,128)(2,1)} async-done(((bf16[32,18,4096]{2,1,0:T(8,128)(2,1)}), bf16[32,18,4096]{2,1,0:T(8,128)(2,1)}, u32[]{:S(2)}, u32[]{:S(2)}) %all-to-all-start.2) | async-done | bytes 4718624 | tf_op jit(solution)/shard_map/all_to_all | solution.py:50
  700.6 4.4 bitcast_reduce_fusion.1
  707.3 3.9 fusion.2
  711.2 7.1 collective-permute-start
  718.3 44.2 %collective-permute-done = bf16[1,128,4096]{2,1,0:T(8,128)(2,1)} collective-permute-done((bf16[1,128,4096]{2,1,0:T(8,128)(2,1)S(1)}, bf16[1,128,4096]{2,1,0:T(8,128)(2,1)}, u32[]{:S(2)}, u32[]{:S(2)}) %collective-permute-start) | collective-permute-done | bytes 1048608 | tf_op jit(solution)/shard_map/ppermute | solution.py:26
  (65 shorter events, 34.8 us)
Async XLA Ops:
  7.2 230.2 %copy-start = (bf16[1,4096,384]{2,1,0:T(8,128)(2,1)S(1)}, bf16[1,4096,384]{2,1,0:T(8,128)(2,1)}, u32[]{:S(2)}) copy-start(bf16[1,4096,384]{2,1,0:T(8,128)(2,1)} %param.13) | copy-start | bytes 9437188
  10.5 4.8 copy-start.13
  10.5 8.0 %copy-start.11 = (f32[1,4096]{1,0:T(1,128)S(1)}, f32[1,4096]{1,0:T(1,128)}, u32[]{:S(2)}) copy-start(f32[1,4096]{1,0:T(1,128)} %param.10) | copy-start | bytes 49156
  10.5 41.8 %all-to-all-start.1 = ((bf16[4,384,1024]{2,1,0:T(8,128)(2,1)}), bf16[4,384,1024]{2,1,0:T(8,128)(2,1)}, u32[]{:S(2)}, u32[]{:S(2)}) async-start(bf16[4,384,1024]{2,1,0:T(8,128)(2,1)} %stack.3), calls=%async_computation.1 | async-start | bytes 6291456 | tf_op jit(solution)/shard_map/all_to_all | solution.py:15
  57.7 9.6 %copy-start.14 = (f32[1,128,2]{1,2,0:T(2,128)S(1)}, f32[1,128,2]{1,2,0:T(2,128)}, u32[]{:S(2)}) copy-start(f32[1,128,2]{1,2,0:T(2,128)} %param.12) | copy-start | bytes 3076
  57.7 145.9 %all-to-all-start = ((bf16[32,18,4096]{2,1,0:T(8,128)(2,1)}), bf16[32,18,4096]{2,1,0:T(8,128)(2,1)}, u32[]{:S(2)}, u32[]{:S(2)}) async-start(bf16[32,18,4096]{2,1,0:T(8,128)(2,1)} %bitcast.79), calls=%async_computation | async-start | bytes 12582912 | tf_op jit(solution)/shard_map/all_to_all | solution.py:44
  67.3 2.2 copy-start.3
  208.9 9.7 %copy-start.12 = (f32[1,384]{1,0:T(1,128)S(1)}, f32[1,384]{1,0:T(1,128)}, u32[]{:S(2)}) copy-start(f32[1,384]{1,0:T(1,128)} %param.15) | copy-start | bytes 4612
  208.9 145.8 %all-to-all-start.3 = ((bf16[32,18,4096]{2,1,0:T(8,128)(2,1)}), bf16[32,18,4096]{2,1,0:T(8,128)(2,1)}, u32[]{:S(2)}, u32[]{:S(2)}) async-start(bf16[32,18,4096]{2,1,0:T(8,128)(2,1)} %bitcast.80), calls=%async_computation.3 | async-start | bytes 12582912 | tf_op jit(solution)/shard_map/all_to_all | solution.py:44
  230.4 7.0 copy-start.5
  362.4 10.4 %copy-start.7 = (f32[576,384]{1,0:T(8,128)S(1)}, f32[576,384]{1,0:T(8,128)}, u32[]{:S(2)}) copy-start(f32[576,384]{1,0:T(8,128)} %fusion.4) | copy-start | bytes 2654212
  362.4 10.4 %copy-start.8 = (f32[576,384]{1,0:T(8,128)S(1)}, f32[576,384]{1,0:T(8,128)}, u32[]{:S(2)}) copy-start(f32[576,384]{1,0:T(8,128)} %fusion.8) | copy-start | bytes 2654212
  372.7 2.7 copy-start.9
  372.7 2.7 copy-start.6
  387.4 145.4 %all-to-all-start.4 = ((bf16[32,18,4096]{2,1,0:T(8,128)(2,1)}), bf16[32,18,4096]{2,1,0:T(8,128)(2,1)}, u32[]{:S(2)}, u32[]{:S(2)}) async-start(bf16[32,18,4096]{2,1,0:T(8,128)(2,1)} %convert_element_type.101), calls=%async_computation.4 | async-start | bytes 12582912 | tf_op jit(solution)/shard_map/all_to_all | solution.py:50
  416.4 125.7 %copy-start.10 = (bf16[576,384]{1,0:T(8,128)(2,1)S(1)}, bf16[576,384]{1,0:T(8,128)(2,1)}, u32[]{:S(2)}) copy-start(bf16[576,384]{1,0:T(8,128)(2,1)} %copy-done.9) | copy-start | bytes 1327108
  532.8 167.7 %all-to-all-start.2 = ((bf16[32,18,4096]{2,1,0:T(8,128)(2,1)}), bf16[32,18,4096]{2,1,0:T(8,128)(2,1)}, u32[]{:S(2)}, u32[]{:S(2)}) async-start(bf16[32,18,4096]{2,1,0:T(8,128)(2,1)} %copy.29), calls=%async_computation.2 | async-start | bytes 12582912 | tf_op jit(solution)/shard_map/all_to_all | solution.py:50
  541.9 220.7 %reduce-scatter.2.cloned.1.call-start = ((), (), s32[]{:S(2)}) async-start(), calls=%async_computation.6 | async-start | bytes 3932160 | tf_op jit(solution)/shard_map/reduce_scatter | solution.py:154
  556.3 4.6 copy-start.2
  560.9 2.6 copy-start.4
  565.4 152.9 %collective-permute-start.1 = (bf16[1,128,4096]{2,1,0:T(8,128)(2,1)}, bf16[1,128,4096]{2,1,0:T(8,128)(2,1)}, u32[]{:S(2)}, u32[]{:S(2)}) collective-permute-start(bf16[1,128,4096]{2,1,0:T(8,128)(2,1)} %fusion.20), channel_id=1, source_target_pairs={{128,0},{129,1},{130,2},{131,3},{132,4},{133,5},{134,6},{135,7},{1... | collective-permute-start | bytes 3145736 | tf_op jit(solution)/shard_map/ppermute | solution.py:26
  707.3 59.8 %copy-start.1 = (bf16[1,4096,384]{2,1,0:T(8,128)(2,1)S(1)}, bf16[1,4096,384]{2,1,0:T(8,128)(2,1)}, u32[]{:S(2)}) copy-start(bf16[1,4096,384]{2,1,0:T(8,128)(2,1)} %param.13) | copy-start | bytes 9437188
  711.2 51.3 %collective-permute-start = (bf16[1,128,4096]{2,1,0:T(8,128)(2,1)S(1)}, bf16[1,128,4096]{2,1,0:T(8,128)(2,1)}, u32[]{:S(2)}, u32[]{:S(2)}) collective-permute-start(bf16[1,128,4096]{2,1,0:T(8,128)(2,1)S(1)} %fusion.2), channel_id=1, source_target_pairs={{0,128},{1,129},{2,130},{3,131},{4,132},{5,133},{6,134},{7,135},{8... | collective-permute-start | bytes 3145736 | tf_op jit(solution)/shard_map/ppermute | solution.py:26
Sparse Core Ops, SparseCore 0:
  549.5 38.9 reduce-scatter.1
